TPU v7x, 32 devices: a whole 2x2x4 slice. The times are simulated.
32 devices in a mesh: groups: 2 (over y), row: 4 (over z), col: 4 (over x, core).
Axes of the slice: x: 2, y: 2, z: 4, core: 2. Of those that a mesh axis runs over, the one named last changes fastest.
Arguments:
- tokens: bfloat16 [512, 8192], P(('groups', 'row'), 'col'), parts along dimension 0, may hold values from -6 to 6
- codes_gate: bfloat16 [8192, 28672], P('col', 'row'), may hold values from 0 to 3, as said below
- codes_up: bfloat16 [8192, 28672], P('col', 'row'), may hold values from 0 to 3, as said below
- scale_gate: float32 [64, 28672], P('col', 'row'), may hold values from 0.003 to 0.03
- offset_gate: float32 [64, 28672], P('col', 'row'), may hold values from 0 to 0.03
- scale_up: float32 [64, 28672], P('col', 'row'), may hold values from 0.003 to 0.03
- offset_up: float32 [64, 28672], P('col', 'row'), may hold values from 0 to 0.03
- grad_hidden: bfloat16 [512, 28672], P(('groups', 'col'), 'row'), parts along dimension 0, may hold values from -0.046875 to 0.046875
Outputs:
- hidden: bfloat16 [512, 28672], P(('groups', 'col'), 'row'), parts along dimension 0
- grad_scale_gate: float32 [128, 28672], P(('groups', 'col'), 'row'), parts along dimension 0
- grad_offset_gate: float32 [128, 28672], P(('groups', 'col'), 'row'), parts along dimension 0
- grad_scale_up: float32 [128, 28672], P(('groups', 'col'), 'row'), parts along dimension 0
- grad_offset_up: float32 [128, 28672], P(('groups', 'col'), 'row'), parts along dimension 0
There are 2 independent parts, one for each index of `groups`. A program takes and returns all parts, laid end to end along the dimension named above; an argument that names none is the same for every part. Nothing has to cross between parts.
Inputs may be any that keep to these rules, and one draw needn't show every extreme that they name: `codes_gate`: whole numbers held as bfloat16. `codes_up`: whole numbers held as bfloat16.
All inputs are finite; a program needn't handle non-finite values.
Results may differ from a plain program's by a relative error of at most 0.006.
Values may be sent and summed in bfloat16 or wider, within the bound.
A program may use at most 256 MiB of HBM per device.

v0:
```python
import jax
import jax.numpy as jnp
from jax import lax
from jax.sharding import PartitionSpec as P

GROUP = 128


def dequant(code_tile, scale_tile, offset):
    levels = code_tile.astype(jnp.float32).reshape(-1, GROUP, code_tile.shape[1])
    weight = levels * scale_tile[:, None, :] - offset[:, None, :]
    return weight.reshape(code_tile.shape).astype(jnp.bfloat16)


def group_grads(wgrad, code_tile):
    levels = code_tile.astype(jnp.float32).reshape(-1, GROUP, code_tile.shape[1])
    grouped = wgrad.reshape(levels.shape)
    return (jnp.sum(grouped * levels, axis=1), -jnp.sum(grouped, axis=1))


def contract(left, right):
    return lax.dot_general(
        left, right, (((0,), (0,)), ((), ())), preferred_element_type=jnp.float32
    )


def local_grads(gate_sum, up_sum, cotangent):
    sigmoid_gate = jax.nn.sigmoid(gate_sum)
    activation = gate_sum * sigmoid_gate
    hidden = (activation * up_sum).astype(jnp.bfloat16)
    slope_term = sigmoid_gate * (1.0 + gate_sum * (1.0 - sigmoid_gate))
    upstream = cotangent.astype(jnp.float32)
    grad_gate = (upstream * up_sum * slope_term).astype(jnp.bfloat16)
    grad_up = (upstream * activation).astype(jnp.bfloat16)
    return (hidden, grad_gate, grad_up)


def on_device(
    tokens, codes_gate, codes_up, scale_gate, offset_gate, scale_up, offset_up, grad_hidden
):
    gathered = lax.all_gather(tokens, "row", axis=0, tiled=True)
    w_gate = dequant(codes_gate, scale_gate, offset_gate)
    w_up = dequant(codes_up, scale_up, offset_up)
    row_count = grad_hidden.shape[0]
    gate_part = jnp.dot(gathered, w_gate, preferred_element_type=jnp.float32)
    up_part = jnp.dot(gathered, w_up, preferred_element_type=jnp.float32)
    gate_sum, up_sum = lax.psum((gate_part, up_part), "col")
    cotangent = lax.all_gather(grad_hidden, "col", axis=0, tiled=True)
    hidden_all, grad_gate, grad_up = local_grads(gate_sum, up_sum, cotangent)
    first_row = lax.axis_index("col") * row_count
    hidden = lax.dynamic_slice_in_dim(hidden_all, first_row, row_count, 0)
    wgrad_gate = contract(gathered, grad_gate)
    wgrad_up = contract(gathered, grad_up)
    scale_g, offset_g = group_grads(wgrad_gate, codes_gate)
    scale_u, offset_u = group_grads(wgrad_up, codes_up)
    return (hidden, scale_g, offset_g, scale_u, offset_u)


def solution(mesh):
    placed = (
        P(("groups", "row"), "col"),
        P("col", "row"),
        P("col", "row"),
        P("col", "row"),
        P("col", "row"),
        P("col", "row"),
        P("col", "row"),
        P(("groups", "col"), "row"),
    )
    return jax.shard_map(
        on_device,
        mesh=mesh,
        in_specs=placed,
        out_specs=(
            P(("groups", "col"), "row"),
            P(("groups", "col"), "row"),
            P(("groups", "col"), "row"),
            P(("groups", "col"), "row"),
            P(("groups", "col"), "row"),
        ),
        check_vma=False,
    )
```

profile of v0, /device:TPU:0, one launch (start us, length us, event | category | flops | bytes accessed | tf_op | source)
XLA Modules:
  0.0 414.2 jit_solution(3010307876142286028)
XLA Ops:
  7.2 0.0 all-gather.3.cloned.1.call-start
  7.2 0.7 all-gather.3.cloned.1.call-update
  7.9 0.0 all-gather.5.cloned.1.call-start
  7.9 0.7 all-gather.5.cloned.1.call-update
  8.7 0.0 copy-start.1
  8.7 0.0 copy-start.2
  8.7 0.0 all-reduce.3.cloned.1.call-start
  8.7 21.3 %fusion = bf16[2048,7168]{1,0:T(8,128)(2,1)} fusion(f32[16,7168]{1,0:T(8,128)} %param.14, f32[16,7168]{1,0:T(8,128)} %param.13, bf16[2048,7168]{1,0:T(8,128)(2,1)} %param.10), kind=kLoop, calls=%fused_computation.3 | loop fusion | flops 58720256 | bytes 59637760 | tf_op jit(solution)/shard_map/convert_element_type | solution.py:12
  30.0 0.0 copy-done.1
  30.0 0.0 copy-done.2
  30.0 21.2 %fusion.1 = bf16[2048,7168]{1,0:T(8,128)(2,1)} fusion(f32[16,7168]{1,0:T(8,128)S(1)} %copy-done.1, f32[16,7168]{1,0:T(8,128)S(1)} %copy-done.2, bf16[2048,7168]{1,0:T(8,128)(2,1)} %param.9), kind=kLoop, calls=%fused_computation.6 | loop fusion | flops 58720256 | bytes 59637760 | tf_op jit(solution)/shard_map/convert_element_type | solution.py:12
  51.2 0.0 all-gather.3.cloned.1.call-done
  51.2 0.0 copy-start.3
  51.2 15.7 %convolution_bitcast_fusion = f32[256,7168]{0,1:T(8,128)} fusion(bf16[2048,7168]{1,0:T(8,128)(2,1)} %fusion, bf16[256,2048]{1,0:T(8,128)(2,1)} %all-gather.3.cloned.1.call-done), kind=kOutput, calls=%fused_computation.10 | convolution fusion | flops 7516192768 | bytes 37748736 | tf_op jit(solution)/shard_map/dot_general | solution.py:46
  66.9 0.0 copy-done.3
  66.9 16.6 %convolution_bitcast_fusion.1 = f32[256,7168]{0,1:T(8,128)} fusion(bf16[2048,7168]{1,0:T(8,128)(2,1)} %fusion.1, bf16[256,2048]{1,0:T(8,128)(2,1)S(1)} %copy-done.3), kind=kOutput, calls=%fused_computation.11 | convolution fusion | flops 7516192768 | bytes 37748736 | tf_op jit(solution)/shard_map/dot_general | solution.py:45
  83.5 0.0 all-reduce.3.cloned.1.call-update
  83.5 0.0 all-gather.5.cloned.1.call-done
  83.5 5.9 %copy.15 = bf16[256,7168]{0,1:T(8,128)(2,1)} copy(bf16[256,7168]{1,0:T(8,128)(2,1)} %all-gather.5.cloned.1.call-done) | data formatting | bytes 7340032 | tf_op jit(solution)/shard_map/all_gather | solution.py:48
  89.4 252.3 %all-reduce.3.cloned.1.call-done = (f32[256,7168]{0,1:T(8,128)}, f32[256,7168]{0,1:T(8,128)}) async-done(((f32[256,7168]{0,1:T(8,128)}, f32[256,7168]{0,1:T(8,128)}), (f32[256,7168]{0,1:T(8,128)}, f32[256,7168]{0,1:T(8,128)})) %all-reduce.3.cloned.1.call-update) | async-done | bytes 14680080 | tf_op jit(solution)/shard_map/psum | solution.py:47
  341.7 0.0 copy-start
  341.7 5.1 %fusion.5 = f32[256,7168]{0,1:T(8,128)S(1)} fusion(f32[256,7168]{0,1:T(8,128)} %get-tuple-element.20), kind=kLoop, calls=%fused_computation.18 | loop fusion | flops 7340032 | bytes 14680064 | tf_op jit(solution)/shard_map/mul | solution.py:29
  346.8 0.0 copy-done
  346.9 2.0 fusion.10
  348.8 1.5 copy.16
  350.3 30.6 %bitcast_reduce_fusion.1 = (f32[16,7168]{1,0:T(8,128)S(1)}, f32[16,7168]{1,0:T(8,128)}) fusion(bf16[2048,7168]{1,0:T(8,128)(2,1)} %param.9, bf16[256,2048]{1,0:T(8,128)(2,1)S(1)} %copy-done.3, f32[256,7168]{0,1:T(8,128)} %get-tuple-element.19, bf16[256,7168]{0,1:T(8,128)(2,1)} %copy.15, f32[256,7168]{0,1:T(8,128)} %get-tuple-element.20), kind=kOutput, calls=%fused_computation.1 | convolution fusion | flops 7594868736 | bytes 49676288 | tf_op jit(solution)/shard_map/dot_general | solution.py:22
  381.0 0.8 neg.10
  381.8 25.1 %bitcast_reduce_fusion = (f32[16,7168]{1,0:T(8,128)S(1)}, f32[16,7168]{1,0:T(8,128)}) fusion(bf16[2048,7168]{1,0:T(8,128)(2,1)} %param.10, bf16[256,2048]{1,0:T(8,128)(2,1)S(1)} %copy-done.3, bf16[256,7168]{0,1:T(8,128)(2,1)} %copy.15, f32[256,7168]{0,1:T(8,128)} %get-tuple-element.20), kind=kOutput, calls=%fused_computation | convolution fusion | flops 7587528704 | bytes 42336256 | tf_op jit(solution)/shard_map/dot_general | solution.py:22
  406.9 0.8 neg.11
Async XLA Ops:
  7.2 44.0 %all-gather.3.cloned.1.call-start = ((), (), s32[]{:S(2)}) async-start(), calls=%async_computation | async-start | bytes 1310720 | tf_op jit(solution)/shard_map/all_gather | solution.py:41
  7.9 75.6 %all-gather.5.cloned.1.call-start = ((), (), s32[]{:S(2)}) async-start(), calls=%async_computation.1 | async-start | bytes 4587520 | tf_op jit(solution)/shard_map/all_gather | solution.py:48
  8.7 21.3 %copy-start.1 = (f32[16,7168]{1,0:T(8,128)S(1)}, f32[16,7168]{1,0:T(8,128)}, u32[]{:S(2)}) copy-start(f32[16,7168]{1,0:T(8,128)} %param.12) | copy-start | bytes 1376260
  8.7 21.3 %copy-start.2 = (f32[16,7168]{1,0:T(8,128)S(1)}, f32[16,7168]{1,0:T(8,128)}, u32[]{:S(2)}) copy-start(f32[16,7168]{1,0:T(8,128)} %param.11) | copy-start | bytes 1376260
  8.7 333.0 %all-reduce.3.cloned.1.call-start = ((), (), s32[]{:S(2)}) async-start(), calls=%async_computation.2 | async-start | bytes 29360128 | tf_op jit(solution)/shard_map/psum | solution.py:47
  51.2 15.7 %copy-start.3 = (bf16[256,2048]{1,0:T(8,128)(2,1)S(1)}, bf16[256,2048]{1,0:T(8,128)(2,1)}, u32[]{:S(2)}) copy-start(bf16[256,2048]{1,0:T(8,128)(2,1)} %all-gather.3.cloned.1.call-done) | copy-start | bytes 3145732
  341.7 5.2 %copy-start = (f32[256,7168]{0,1:T(8,128)S(1)}, f32[256,7168]{0,1:T(8,128)}, u32[]{:S(2)}) copy-start(f32[256,7168]{0,1:T(8,128)} %get-tuple-element.19) | copy-start | bytes 22020100
Sparse Core Ops, SparseCore 0:
  9.6 30.6 all-gather.2
  41.8 30.9 all-gather.4
  83.6 258.0 all-reduce.2
where the time goes:
time: 414 us
  waiting for transfers between devices  254 us (61%)
  matrix products  88.1 us (21%)
  other arithmetic  51.1 us (12%)
  between operations  13.8 us (3%)
  local copies, waits for them, and re-layouts  7.49 us (2%)
    psum x1, waiting for transfers between devices, on_device(): gate_sum, up_sum = lax.psum((gate_part, up_part), 'col')  252 us
    dot_general x2, matrix products, contract(): lax.dot_general(left, right, (((0,), (0,)), ((), ())), preferred_element_...  55.8 us
    convert_element_type x2, other arithmetic, dequant(): return weight.reshape(code_tile.shape).astype(jnp.bfloat16)  42.4 us
    dot_general x1, matrix products, on_device(): gate_part = jnp.dot(gathered, w_gate, preferred_element_type=jnp.float32)  16.6 us
    dot_general x1, matrix products, on_device(): up_part = jnp.dot(gathered, w_up, preferred_element_type=jnp.float32)  15.7 us
  transfers between devices with their start and end apart: 3, of which 1 were waited for; matrix products, arithmetic and copies ran while one was open for 19% of the time, Pallas kernels for 0%

commit v1 on v0

v1 whole, which is shorter than its diff:
```python
import functools

import jax
import jax.numpy as jnp
from jax import lax
from jax.experimental import pallas as pl
from jax.experimental.pallas import tpu as pltpu
from jax.sharding import PartitionSpec as P

GROUP = 128
MESH = pl.DeviceIdType.MESH


def body(
    dims,
    tokens_ref, fwd_gate, fwd_up, scale_gate, offset_gate, scale_up, offset_up,
    cot_ref, bwd_gate, bwd_up,
    hidden_ref, gs_gate, go_gate, gs_up, go_up,
    tok, tok_t, acc, core_out, core_in, x_out, x_in, mine, grads,
    tok_send, tok_recv, core_send, core_recv, x_send, x_recv,
    ag_send, ag_recv, mate_send, mate_recv,
):
    Z, X, J, rows, width = dims
    step = pl.program_id(0)
    z = lax.axis_index("row")
    col = lax.axis_index("col")
    x, c = col // 2, lax.rem(col, 2)
    mate = x * 2 + 1 - c
    z_rows, depth = tokens_ref.shape
    total = Z * z_rows

    def peer(o):
        return lax.rem(x + o, X)

    def to(src, dst, send, recv, axis, index):
        return pltpu.make_async_remote_copy(
            src_ref=src, dst_ref=dst, send_sem=send, recv_sem=recv,
            device_id={axis: index}, device_id_type=MESH,
        )

    def token_copy(o):
        place = pl.ds(pl.multiple_of(z * z_rows, z_rows), z_rows)
        return to(tokens_ref, tok.at[place, :], tok_send.at[o - 1], tok_recv.at[o - 1],
                  "row", lax.rem(z + o, Z))

    def core_copy(j):
        return to(core_out.at[j], core_in.at[j], core_send.at[j], core_recv.at[j], "col", mate)

    def x_copy(j, o):
        return to(x_out.at[j, o - 1], x_in.at[j, o - 1], x_send.at[j, o - 1],
                  x_recv.at[j, o - 1], "col", peer(o) * 2 + c)

    def grad_copy(j, o):
        block = grads.at[j, x * 2 + c]
        return to(block, block, ag_send.at[j, o - 1], ag_recv.at[j, o - 1],
                  "col", peer(o) * 2 + c)

    def mate_copy(j, o):
        block = grads.at[j, lax.rem(x + X - o, X) * 2 + c]
        return to(block, block, mate_send.at[j, o], mate_recv.at[j, o], "col", mate)

    @pl.when(step == 0)
    def _():
        barrier = pltpu.get_barrier_semaphore()
        for o in range(1, Z):
            pl.semaphore_signal(barrier, inc=1, device_id={"row": lax.rem(z + o, Z)},
                                device_id_type=MESH)
        for o in range(1, X):
            pl.semaphore_signal(barrier, inc=1, device_id={"col": peer(o) * 2 + c},
                                device_id_type=MESH)
        pl.semaphore_signal(barrier, inc=1, device_id={"col": mate}, device_id_type=MESH)
        pl.semaphore_wait(barrier, Z + X - 1)
        for o in range(1, Z):
            token_copy(o).start()
        tok[pl.ds(pl.multiple_of(z * z_rows, z_rows), z_rows), :] = tokens_ref[...]
        for o in range(1, Z):
            token_copy(o).wait()
        for k in range(0, depth, 512):
            tok_t[k:k + 512, :] = tok[:, k:k + 512].astype(jnp.float32).T.astype(jnp.bfloat16)

    @pl.when((step >= 1) & (step < J + 1))
    def _():
        j = step - 1
        slot = lax.rem(j, 2)
        core_copy(j).wait_recv()
        for o in range(1, X):
            xp = peer(o)
            for m in range(2):
                x_out[j, o - 1, m] = (
                    acc[slot, m, xp * 2 + c] + core_in[j, m, xp].astype(jnp.float32)
                ).astype(jnp.bfloat16)
            x_copy(j, o).start()
        for m in range(2):
            mine[slot, m] = acc[slot, m, x * 2 + c] + core_in[j, m, x].astype(jnp.float32)

    @pl.when((step >= 2) & (step < J + 2))
    def _():
        j = step - 2
        slot = lax.rem(j, 2)
        gate, up = mine[slot, 0], mine[slot, 1]
        for o in range(1, X):
            x_copy(j, o).wait_recv()
            gate = gate + x_in[j, o - 1, 0].astype(jnp.float32)
            up = up + x_in[j, o - 1, 1].astype(jnp.float32)
        sigmoid = jax.nn.sigmoid(gate)
        activation = gate * sigmoid
        hidden_ref[...] = (activation * up).astype(jnp.bfloat16)
        upstream = cot_ref[...].astype(jnp.float32)
        slope = sigmoid * (1.0 + gate * (1.0 - sigmoid))
        grads[j, col, 0] = (upstream * up * slope).astype(jnp.bfloat16)
        grads[j, col, 1] = (upstream * activation).astype(jnp.bfloat16)
        for o in range(1, X):
            grad_copy(j, o).start()
        mate_copy(j, 0).start()

    @pl.when(step < J)
    def _():
        j = step
        slot = lax.rem(j, 2)
        for m, (codes, scale, offset) in enumerate(
            ((fwd_gate, scale_gate, offset_gate), (fwd_up, scale_up, offset_up))
        ):
            part = None
            for k in range(0, depth, 512):
                pieces = []
                for g in range(k // GROUP, (k + 512) // GROUP):
                    levels = codes[g * GROUP:(g + 1) * GROUP, :].astype(jnp.float32)
                    pieces.append(
                        (levels * scale[g:g + 1, :] - offset[g:g + 1, :]).astype(jnp.bfloat16)
                    )
                term = jnp.dot(tok[:, k:k + 512], jnp.concatenate(pieces, axis=0),
                               preferred_element_type=jnp.float32)
                part = term if part is None else part + term
            acc[slot, m] = part.reshape(2 * X, rows, width)
            for xp in range(X):
                core_out[j, m, xp] = acc[slot, m, xp * 2 + 1 - c].astype(jnp.bfloat16)
        core_copy(j).start()

    @pl.when(step >= 4)
    def _():
        j = step - 4
        for o in range(X):
            mate_copy(j, o).wait()
        for o in range(1, X):
            x_copy(j, o).wait_send()
            grad_copy(j, o).wait_send()
        core_copy(j).wait_send()
        for m, (codes, gs, go) in enumerate(((bwd_gate, gs_gate, go_gate), (bwd_up, gs_up, go_up))):
            grad = grads[j, :, m].reshape(total, width)
            for k in range(0, depth, 512):
                wgrad = jnp.dot(tok_t[k:k + 512, :], grad, preferred_element_type=jnp.float32)
                levels = codes[k:k + 512, :].astype(jnp.float32)
                count = 512 // GROUP
                first = k // GROUP
                gs[first:first + count, :] = jnp.sum(
                    (wgrad * levels).reshape(count, GROUP, width), axis=1)
                go[first:first + count, :] = -jnp.sum(
                    wgrad.reshape(count, GROUP, width), axis=1)

    @pl.when((step >= 3) & (step < J + 3))
    def _():
        j = step - 3
        for o in range(1, X):
            grad_copy(j, o).wait_recv()
            mate_copy(j, o).start()


def solution(mesh):
    Z, X = mesh.shape["row"], mesh.shape["col"] // 2

    def on_device(tokens, codes_gate, codes_up, scale_gate, offset_gate, scale_up, offset_up,
                  grad_hidden):
        z_rows, depth = tokens.shape
        rows, n = grad_hidden.shape
        width = 512 if n % 512 == 0 else 256
        J = n // width
        groups = scale_gate.shape[0]
        total = Z * z_rows
        bf16, f32 = jnp.bfloat16, jnp.float32

        def at(lag):
            return lambda s: (0, jnp.clip(s - lag, 0, J - 1))

        codes_fwd = pl.BlockSpec((depth, width), at(0))
        codes_bwd = pl.BlockSpec((depth, width), at(4))
        steps_fwd = pl.BlockSpec((groups, width), at(0))
        steps_bwd = pl.BlockSpec((groups, width), at(4))
        token_rows = pl.BlockSpec((rows, width), at(2))
        dma = pltpu.SemaphoreType.DMA
        macs = 4 * total * depth * n
        return pl.pallas_call(
            functools.partial(body, (Z, X, J, rows, width)),
            grid=(J + 4,),
            out_shape=[
                jax.ShapeDtypeStruct((rows, n), bf16),
            ] + [jax.ShapeDtypeStruct((groups, n), f32)] * 4,
            in_specs=[
                pl.BlockSpec((z_rows, depth), lambda s: (0, 0)),
                codes_fwd, codes_fwd, steps_fwd, steps_fwd, steps_fwd, steps_fwd,
                token_rows, codes_bwd, codes_bwd,
            ],
            out_specs=[token_rows] + [steps_bwd] * 4,
            scratch_shapes=[
                pltpu.VMEM((total, depth), bf16),
                pltpu.VMEM((depth, total), bf16),
                pltpu.VMEM((2, 2, 2 * X, rows, width), f32),
                pltpu.VMEM((J, 2, X, rows, width), bf16),
                pltpu.VMEM((J, 2, X, rows, width), bf16),
                pltpu.VMEM((J, X - 1, 2, rows, width), bf16),
                pltpu.VMEM((J, X - 1, 2, rows, width), bf16),
                pltpu.VMEM((2, 2, rows, width), f32),
                pltpu.VMEM((J, 2 * X, 2, rows, width), bf16),
                dma((Z - 1,)), dma((Z - 1,)),
                dma((J,)), dma((J,)),
                dma((J, X - 1)), dma((J, X - 1)),
                dma((J, X - 1)), dma((J, X - 1)),
                dma((J, X)), dma((J, X)),
            ],
            compiler_params=pltpu.CompilerParams(
                collective_id=0, has_side_effects=True, vmem_limit_bytes=60 * 1024 * 1024,
            ),
            cost_estimate=pl.CostEstimate(
                flops=2 * macs, bytes_accessed=8 * depth * n, transcendentals=rows * n),
        )(tokens, codes_gate, codes_up, scale_gate, offset_gate, scale_up, offset_up,
          grad_hidden, codes_gate, codes_up)

    rows_by_group = P(("groups", "col"), "row")
    weights = P("col", "row")
    return jax.shard_map(
        on_device,
        mesh=mesh,
        in_specs=(P(("groups", "row"), "col"),) + (weights,) * 6 + (rows_by_group,),
        out_specs=(rows_by_group,) * 5,
        check_vma=False,
    )
```

time: 414 us -> 131 us (0.32)
  the two profiles are of different devices: /device:TPU:0 before, /device:TPU:13 now
where the time goes in v1:
time: 131 us
  Pallas kernels  121 us (92%)
  local copies, waits for them, and re-layouts  9.42 us (7%)
    pallas_call x1, Pallas kernels, on_device(): pl.pallas_call(functools.partial(body, (Z, X, J, rows, width)), grid=(J +...  121 us
    unnamed x5, local copies, waits for them, and re-layouts  9.42 us

profile of v1, /device:TPU:13, one launch (start us, length us, event | category | flops | bytes accessed | tf_op | source)
XLA Modules:
  0.0 130.6 jit_solution(11011167582973843904)
XLA Ops:
  0.6 120.5 %shard_map.119 = (bf16[64,7168]{1,0:T(8,128)(2,1)}, f32[16,7168]{1,0:T(8,128)}, f32[16,7168]{1,0:T(8,128)}, f32[16,7168]{1,0:T(8,128)}, f32[16,7168]{1,0:T(8,128)}) custom-call(bf16[64,2048]{1,0:T(8,128)(2,1)} %tokens_ref.1, bf16[2048,7168]{1,0:T(8,128)(2,1)} %bwd_gate.1, bf16[2048,7168]{1,0:T(8,128)(2,1)} %bwd_up.1, f32[16,7168]{1,0:T(8,128)} %scale_gate.1, ...), custom_call_target="tpu_custom_call" | custom-call | flops 30064771072 | bytes 117440512 | tf_op jit(solution)/shard_map/pallas_call | solution.py:191
  121.2 2.2 %copy.18 = bf16[64,7168]{1,0:T(8,128)(2,1)} copy(bf16[64,7168]{1,0:T(8,128)(2,1)} %get-tuple-element.10) | data formatting | bytes 1835008
  123.3 1.8 %copy.19 = f32[16,7168]{1,0:T(8,128)} copy(f32[16,7168]{1,0:T(8,128)} %get-tuple-element.11) | data formatting | bytes 917504
  125.2 1.8 %copy.20 = f32[16,7168]{1,0:T(8,128)} copy(f32[16,7168]{1,0:T(8,128)} %get-tuple-element.12) | data formatting | bytes 917504
  127.0 1.8 %copy.21 = f32[16,7168]{1,0:T(8,128)} copy(f32[16,7168]{1,0:T(8,128)} %get-tuple-element.13) | data formatting | bytes 917504
  128.8 1.8 %copy.22 = f32[16,7168]{1,0:T(8,128)} copy(f32[16,7168]{1,0:T(8,128)} %get-tuple-element.14) | data formatting | bytes 917504

commit v2 on v1

--- a/solution.py
+++ b/solution.py
@@ -9,6 +9,8 @@
 
 GROUP = 128
 MESH = pl.DeviceIdType.MESH
+ACT, PASS_ON, BACK = 3, 5, 6
+KEPT = 4
 
 
 def body(
@@ -38,10 +40,14 @@
             device_id={axis: index}, device_id_type=MESH,
         )
 
-    def token_copy(o):
-        place = pl.ds(pl.multiple_of(z * z_rows, z_rows), z_rows)
-        return to(tokens_ref, tok.at[place, :], tok_send.at[o - 1], tok_recv.at[o - 1],
-                  "row", lax.rem(z + o, Z))
+    piece = z_rows // 2
+
+    def token_copy(way, h, half, block_of):
+        owner = jnp.clip(block_of - way * h, 0, Z - 1)
+        place = tok.at[pl.ds(pl.multiple_of(owner * z_rows + half * piece, piece), piece), :]
+        lane = 0 if way == 1 else 1
+        return to(place, place, tok_send.at[lane, h, half], tok_recv.at[lane, h, half],
+                  "row", jnp.clip(z + way, 0, Z - 1))
 
     def core_copy(j):
         return to(core_out.at[j], core_in.at[j], core_send.at[j], core_recv.at[j], "col", mate)
@@ -62,19 +68,51 @@
     @pl.when(step == 0)
     def _():
         barrier = pltpu.get_barrier_semaphore()
-        for o in range(1, Z):
-            pl.semaphore_signal(barrier, inc=1, device_id={"row": lax.rem(z + o, Z)},
-                                device_id_type=MESH)
+        for way in (1, -1):
+            @pl.when((z + way >= 0) & (z + way < Z))
+            def _(way=way):
+                pl.semaphore_signal(barrier, inc=1,
+                                    device_id={"row": jnp.clip(z + way, 0, Z - 1)},
+                                    device_id_type=MESH)
         for o in range(1, X):
             pl.semaphore_signal(barrier, inc=1, device_id={"col": peer(o) * 2 + c},
                                 device_id_type=MESH)
         pl.semaphore_signal(barrier, inc=1, device_id={"col": mate}, device_id_type=MESH)
-        pl.semaphore_wait(barrier, Z + X - 1)
-        for o in range(1, Z):
-            token_copy(o).start()
         tok[pl.ds(pl.multiple_of(z * z_rows, z_rows), z_rows), :] = tokens_ref[...]
-        for o in range(1, Z):
-            token_copy(o).wait()
+        ends = jnp.where(z == 0, 1, 0) + jnp.where(z == Z - 1, 1, 0)
+        pl.semaphore_wait(barrier, X + 2 - ends)
+
+        def sends(way, h):
+            return (z - way * h >= 0) & (z - way * h < Z) & (z + way >= 0) & (z + way < Z)
+
+        def takes(way, h):
+            return (z - way * (h + 1) >= 0) & (z - way * (h + 1) < Z)
+
+        for h in range(Z - 1):
+            for half in range(2):
+                for way in (1, -1):
+                    if h:
+                        @pl.when(takes(way, h - 1))
+                        def _(way=way):
+                            token_copy(way, h - 1, half, z - way).wait_recv()
+
+                    @pl.when(sends(way, h))
+                    def _(way=way):
+                        token_copy(way, h, half, z).start()
+        for half in range(2):
+            for way in (1, -1):
+                @pl.when(takes(way, Z - 2))
+                def _(way=way):
+                    token_copy(way, Z - 2, half, z - way).wait_recv()
+
+    @pl.when(step == 2)
+    def _():
+        for way in (1, -1):
+            for h in range(Z - 1):
+                @pl.when((z - way * h >= 0) & (z - way * h < Z) & (z + way >= 0) & (z + way < Z))
+                def _(way=way, h=h):
+                    for half in range(2):
+                        token_copy(way, h, half, z).wait_send()
         for k in range(0, depth, 512):
             tok_t[k:k + 512, :] = tok[:, k:k + 512].astype(jnp.float32).T.astype(jnp.bfloat16)
 
@@ -91,12 +129,12 @@
                 ).astype(jnp.bfloat16)
             x_copy(j, o).start()
         for m in range(2):
-            mine[slot, m] = acc[slot, m, x * 2 + c] + core_in[j, m, x].astype(jnp.float32)
-
-    @pl.when((step >= 2) & (step < J + 2))
-    def _():
-        j = step - 2
-        slot = lax.rem(j, 2)
+            mine[lax.rem(j, KEPT), m] = acc[slot, m, x * 2 + c] + core_in[j, m, x].astype(jnp.float32)
+
+    @pl.when((step >= ACT) & (step < J + ACT))
+    def _():
+        j = step - ACT
+        slot = lax.rem(j, KEPT)
         gate, up = mine[slot, 0], mine[slot, 1]
         for o in range(1, X):
             x_copy(j, o).wait_recv()
@@ -136,9 +174,9 @@
                 core_out[j, m, xp] = acc[slot, m, xp * 2 + 1 - c].astype(jnp.bfloat16)
         core_copy(j).start()
 
-    @pl.when(step >= 4)
-    def _():
-        j = step - 4
+    @pl.when(step >= BACK)
+    def _():
+        j = step - BACK
         for o in range(X):
             mate_copy(j, o).wait()
         for o in range(1, X):
@@ -157,12 +195,17 @@
                 go[first:first + count, :] = -jnp.sum(
                     wgrad.reshape(count, GROUP, width), axis=1)
 
-    @pl.when((step >= 3) & (step < J + 3))
-    def _():
-        j = step - 3
+    @pl.when((step >= PASS_ON) & (step < J + PASS_ON))
+    def _():
+        j = step - PASS_ON
         for o in range(1, X):
             grad_copy(j, o).wait_recv()
             mate_copy(j, o).start()
+
+
+def deliver(*refs):
+    for i in range(5):
+        refs[5 + i][...] = refs[i][...]
 
 
 def solution(mesh):
@@ -172,7 +215,7 @@
                   grad_hidden):
         z_rows, depth = tokens.shape
         rows, n = grad_hidden.shape
-        width = 512 if n % 512 == 0 else 256
+        width = 256
         J = n // width
         groups = scale_gate.shape[0]
         total = Z * z_rows
@@ -182,15 +225,15 @@
             return lambda s: (0, jnp.clip(s - lag, 0, J - 1))
 
         codes_fwd = pl.BlockSpec((depth, width), at(0))
-        codes_bwd = pl.BlockSpec((depth, width), at(4))
+        codes_bwd = pl.BlockSpec((depth, width), at(BACK))
         steps_fwd = pl.BlockSpec((groups, width), at(0))
-        steps_bwd = pl.BlockSpec((groups, width), at(4))
-        token_rows = pl.BlockSpec((rows, width), at(2))
+        steps_bwd = pl.BlockSpec((groups, width), at(BACK))
+        token_rows = pl.BlockSpec((rows, width), at(ACT))
         dma = pltpu.SemaphoreType.DMA
         macs = 4 * total * depth * n
-        return pl.pallas_call(
+        results = pl.pallas_call(
             functools.partial(body, (Z, X, J, rows, width)),
-            grid=(J + 4,),
+            grid=(J + BACK,),
             out_shape=[
                 jax.ShapeDtypeStruct((rows, n), bf16),
             ] + [jax.ShapeDtypeStruct((groups, n), f32)] * 4,
@@ -208,9 +251,9 @@
                 pltpu.VMEM((J, 2, X, rows, width), bf16),
                 pltpu.VMEM((J, X - 1, 2, rows, width), bf16),
                 pltpu.VMEM((J, X - 1, 2, rows, width), bf16),
-                pltpu.VMEM((2, 2, rows, width), f32),
+                pltpu.VMEM((KEPT, 2, rows, width), f32),
                 pltpu.VMEM((J, 2 * X, 2, rows, width), bf16),
-                dma((Z - 1,)), dma((Z - 1,)),
+                dma((2, Z - 1, 2)), dma((2, Z - 1, 2)),
                 dma((J,)), dma((J,)),
                 dma((J, X - 1)), dma((J, X - 1)),
                 dma((J, X - 1)), dma((J, X - 1)),
@@ -223,6 +266,15 @@
                 flops=2 * macs, bytes_accessed=8 * depth * n, transcendentals=rows * n),
         )(tokens, codes_gate, codes_up, scale_gate, offset_gate, scale_up, offset_up,
           grad_hidden, codes_gate, codes_up)
+        part = n // 7
+        blocks = [pl.BlockSpec((r.shape[0], part), lambda s: (0, s)) for r in results]
+        return pl.pallas_call(
+            deliver,
+            grid=(7,),
+            out_shape=[jax.ShapeDtypeStruct(r.shape, r.dtype) for r in results],
+            in_specs=blocks,
+            out_specs=blocks,
+        )(*results)
 
     rows_by_group = P(("groups", "col"), "row")
     weights = P("col", "row")

time: 131 us -> 122 us (0.931)
  the two profiles are of different devices: /device:TPU:13 before, /device:TPU:0 now
where the time goes in v2:
time: 122 us; the launch traced here: 121 us
  Pallas kernels  121 us (99%)
    pallas_call x1, Pallas kernels, on_device(): pl.pallas_call(functools.partial(body, (Z, X, J, rows, width)), grid=(J +...  115 us
    pallas_call x1, Pallas kernels, on_device(): pl.pallas_call(deliver, grid=(7,), out_shape=[jax.ShapeDtypeStruct(r.shap...  5.5 us

profile of v2, /device:TPU:0, one launch (start us, length us, event | category | flops | bytes accessed | tf_op | source)
XLA Modules:
  0.0 121.4 jit_solution(6420062006976717608)
XLA Ops:
  0.6 115.2 %shard_map.119 = (bf16[64,7168]{1,0:T(8,128)(2,1)}, f32[16,7168]{1,0:T(8,128)}, f32[16,7168]{1,0:T(8,128)}, f32[16,7168]{1,0:T(8,128)}, f32[16,7168]{1,0:T(8,128)}) custom-call(bf16[64,2048]{1,0:T(8,128)(2,1)} %tokens_ref.1, bf16[2048,7168]{1,0:T(8,128)(2,1)} %bwd_gate.1, bf16[2048,7168]{1,0:T(8,128)(2,1)} %bwd_up.1, f32[16,7168]{1,0:T(8,128)} %scale_gate.1, ...), custom_call_target="tpu_custom_call" | custom-call | flops 30064771072 | bytes 117440512 | tf_op jit(solution)/shard_map/pallas_call | solution.py:234
  115.9 5.5 %shard_map.120 = (bf16[64,7168]{1,0:T(8,128)(2,1)}, f32[16,7168]{1,0:T(8,128)}, f32[16,7168]{1,0:T(8,128)}, f32[16,7168]{1,0:T(8,128)}, f32[16,7168]{1,0:T(8,128)}) custom-call(bf16[64,7168]{1,0:T(8,128)(2,1)} %get-tuple-element.10.refs_0_, f32[16,7168]{1,0:T(8,128)} %get-tuple-element.11.refs_1_, f32[16,7168]{1,0:T(8,128)} %get-tuple-element.12.refs_2_, ...), custom_call_target="tpu_custom_call" | custom-call | tf_op jit(solution)/shard_map/pallas_call | solution.py:271

commit v3 on v2

--- a/solution.py
+++ b/solution.py
@@ -9,7 +9,7 @@
 
 GROUP = 128
 MESH = pl.DeviceIdType.MESH
-ACT, PASS_ON, BACK = 3, 5, 6
+ACT, PASS_ON, BACK = 2, 4, 5
 KEPT = 4
 
 
@@ -266,11 +266,11 @@
                 flops=2 * macs, bytes_accessed=8 * depth * n, transcendentals=rows * n),
         )(tokens, codes_gate, codes_up, scale_gate, offset_gate, scale_up, offset_up,
           grad_hidden, codes_gate, codes_up)
-        part = n // 7
+        part = n // 2
         blocks = [pl.BlockSpec((r.shape[0], part), lambda s: (0, s)) for r in results]
         return pl.pallas_call(
             deliver,
-            grid=(7,),
+            grid=(2,),
             out_shape=[jax.ShapeDtypeStruct(r.shape, r.dtype) for r in results],
             in_specs=blocks,
             out_specs=blocks,

time: 122 us -> 121 us (level)
    pallas_call x1, Pallas kernels: 5.5 us -> 3.01 us  [on_device(): pl.pallas_call(deliver, grid=(2,), out_shape=[jax.ShapeDtypeStruct(r.shap...]
    pallas_call x1, Pallas kernels: 115 us -> 117 us  [on_device(): pl.pallas_call(functools.partial(body, (Z, X, J, rows, width)), grid=(J +...]
where the time goes in v3:
time: 121 us
  Pallas kernels  120 us (99%)
    pallas_call x1, Pallas kernels, on_device(): pl.pallas_call(functools.partial(body, (Z, X, J, rows, width)), grid=(J +...  117 us
    pallas_call x1, Pallas kernels, on_device(): pl.pallas_call(deliver, grid=(2,), out_shape=[jax.ShapeDtypeStruct(r.shap...  3.01 us

profile of v3, /device:TPU:0, one launch (start us, length us, event | category | flops | bytes accessed | tf_op | source)
XLA Modules:
  0.0 120.8 jit_solution(14007493880641411361)
XLA Ops:
  0.6 117.1 %shard_map.119 = (bf16[64,7168]{1,0:T(8,128)(2,1)}, f32[16,7168]{1,0:T(8,128)}, f32[16,7168]{1,0:T(8,128)}, f32[16,7168]{1,0:T(8,128)}, f32[16,7168]{1,0:T(8,128)}) custom-call(bf16[64,2048]{1,0:T(8,128)(2,1)} %tokens_ref.1, bf16[2048,7168]{1,0:T(8,128)(2,1)} %bwd_gate.1, bf16[2048,7168]{1,0:T(8,128)(2,1)} %bwd_up.1, f32[16,7168]{1,0:T(8,128)} %scale_gate.1, ...), custom_call_target="tpu_custom_call" | custom-call | flops 30064771072 | bytes 117440512 | tf_op jit(solution)/shard_map/pallas_call | solution.py:234
  117.7 3.0 %shard_map.120 = (bf16[64,7168]{1,0:T(8,128)(2,1)}, f32[16,7168]{1,0:T(8,128)}, f32[16,7168]{1,0:T(8,128)}, f32[16,7168]{1,0:T(8,128)}, f32[16,7168]{1,0:T(8,128)}) custom-call(bf16[64,7168]{1,0:T(8,128)(2,1)} %get-tuple-element.10.refs_0_, f32[16,7168]{1,0:T(8,128)} %get-tuple-element.11.refs_1_, f32[16,7168]{1,0:T(8,128)} %get-tuple-element.12.refs_2_, ...), custom_call_target="tpu_custom_call" | custom-call | tf_op jit(solution)/shard_map/pallas_call | solution.py:271
